TPU v7x, 32 devices: a whole 2x2x4 slice. The times are simulated.
32 devices in a mesh: grp: 2 (over y), role: 2 (over core), ctx: 8 (over z, x).
Axes of the slice: x: 2, y: 2, z: 4, core: 2. Of those that a mesh axis runs over, the one named last changes fastest.
Arguments:
- teacher_streams: bfloat16 [3, 8192, 4096], P(None, ('grp', 'ctx'), 'role'), parts along dimension 1, may hold values from -6 to 6
- conv_filter: bfloat16 [4096, 128], P('role'), may hold values from -0.5 to 0.5
- map_weight: bfloat16 [4096, 2048], P(('role', 'ctx')), may hold values from -0.125 to 0.125
- bases: int32 [8192], P(('grp', 'ctx')), parts along dimension 0, may hold values from 0 to 3
- base_weights: float32 [4], replicated, may hold values from 0.25 to 2
- student_qkv: bfloat16 [3, 8192, 2048], P(None, ('grp', 'ctx'), 'role'), parts along dimension 1, may hold values from -6 to 6
Outputs:
- student_grads: bfloat16 [3, 8192, 2048], P(None, ('grp', 'ctx'), 'role'), parts along dimension 1
There are 2 independent parts, one for each index of `grp`. A program takes and returns all parts, laid end to end along the dimension named above; an argument that names none is the same for every part. Nothing has to cross between parts.
All inputs are finite; a program needn't handle non-finite values.
Results may differ from a plain program's by a relative error of at most 0.0055.
Values may be sent and summed in bfloat16 or wider, within the bound.
A program may use at most 192 MiB of HBM per device.

v0:
```python
from functools import reduce
import jax
import jax.numpy as jnp
from jax import lax
from jax.sharding import PartitionSpec as P

DH = 128
BLK = 512


def from_behind(value, axis, steps):
    count = lax.axis_size(axis)
    leading, last = (max(0, -steps), min(count, count - steps))
    return lax.ppermute(value, axis, [(source, source + steps) for source in range(leading, last)])


def prefix(value, axis, join, neutral, backward):
    count, mine = (lax.axis_size(axis), lax.axis_index(axis))
    pieces = lax.all_gather(value, axis)
    if backward:
        pieces = pieces[::-1]
        mine = count - 1 - mine
    so_far = jnp.full_like(value, 0) + jnp.asarray(neutral, value.dtype)

    def turn(position, so_far):
        longer = join(so_far, pieces[position])
        return jnp.where(position < mine, longer, so_far)

    return lax.fori_loop(0, count - 1, turn, so_far)


def depthwise(extended, filters):
    kernel = jnp.flip(filters, axis=1).T[:, None, :]
    result = lax.conv_general_dilated(
        extended[None],
        kernel,
        (1,),
        "VALID",
        dimension_numbers=("NWC", "WIO", "NWC"),
        feature_group_count=extended.shape[1],
        preferred_element_type=jnp.float32,
    )
    return result[0]


def add_states(earlier, later):
    return earlier + later


def on_device(teacher_streams, conv_filter, map_weight, bases, base_weights, student_qkv):
    gate_in = teacher_streams[0]
    mixed_in = (
        teacher_streams[1].astype(jnp.float32) * teacher_streams[2].astype(jnp.float32)
    ).astype(jnp.bfloat16)
    tok_rows = mixed_in.shape[0]
    rim_rows = conv_filter.shape[1] - 1
    left_rim = from_behind(mixed_in[tok_rows - rim_rows :], "ctx", 1)
    conv_out = depthwise(jnp.concatenate([left_rim, mixed_in], 0), conv_filter)
    teacher_out = (gate_in.astype(jnp.float32) * conv_out).astype(jnp.bfloat16)
    zero_map = jnp.zeros((tok_rows, map_weight.shape[1]), jnp.float32)
    shard_rows = lax.all_gather(map_weight, "ctx", axis=0, tiled=True)
    columns = lax.slice_in_dim(teacher_out, 0, shard_rows.shape[0], axis=1)
    partial_map = zero_map + jnp.dot(columns, shard_rows, preferred_element_type=jnp.float32)
    target = lax.psum_scatter(partial_map, "role", scatter_dimension=1, tiled=True)
    head_width = student_qkv.shape[2]
    heads_dev = head_width // DH
    queries = student_qkv[0].reshape(tok_rows, heads_dev, DH)
    keys_all = student_qkv[1].reshape(tok_rows, heads_dev, DH)
    values_all = student_qkv[2].reshape(tok_rows, heads_dev, DH)
    att_scale = float(DH * tok_rows * lax.axis_size("ctx")) ** (-0.5)
    nblocks = tok_rows // BLK
    causal = (jnp.arange(BLK)[:, None] >= jnp.arange(BLK)[None, :])[None]
    state_terms = [
        jnp.einsum("shd,she->hde", keys_all, values_all, preferred_element_type=jnp.float32)
    ]
    zero_state = jnp.zeros((heads_dev, DH, DH), jnp.float32)
    own_state = reduce(jnp.add, state_terms)
    carried = prefix(own_state, "ctx", add_states, zero_state, False)
    outputs = []
    block = 0
    prefix_bf = carried.astype(jnp.bfloat16)
    scores = jnp.einsum("thd,shd->hts", queries, keys_all, preferred_element_type=jnp.float32)
    scores_bf = jnp.where(causal, scores, 0.0).astype(jnp.bfloat16)
    block_out = att_scale * (
        jnp.einsum("thd,hde->the", queries, prefix_bf, preferred_element_type=jnp.float32)
        + jnp.einsum("hts,she->the", scores_bf, values_all, preferred_element_type=jnp.float32)
    )
    prefixes = [prefix_bf]
    kept_scores = [scores_bf]
    outputs.append(block_out.reshape(BLK, head_width))
    outputs = outputs[0]
    onehot = (bases[:, None] == jnp.arange(base_weights.shape[0])[None, :]).astype(jnp.float32)
    tok_weight = jnp.sum(onehot * base_weights[None, :], axis=1)
    resid_bf = (
        (tok_weight[:, None] * (outputs - target))
        .astype(jnp.bfloat16)
        .reshape(tok_rows, heads_dev, DH)
    )
    back_terms = [jnp.einsum("thd,the->hde", queries, resid_bf, preferred_element_type=jnp.float32)]
    own_back = reduce(jnp.add, back_terms)
    later_sum = prefix(own_back, "ctx", add_states, zero_state, True)
    grad_blocks = [None] * nblocks
    for block in reversed(range(nblocks)):
        later_bf = later_sum.astype(jnp.bfloat16)
        later_sum = later_sum + back_terms[block]
        scores_bf = kept_scores[block]
        grad_scores = jnp.where(
            causal,
            jnp.einsum("the,she->hts", resid_bf, values_all, preferred_element_type=jnp.float32),
            0.0,
        ).astype(jnp.bfloat16)
        grad_query = att_scale * (
            jnp.einsum(
                "the,hde->thd", resid_bf, prefixes[block], preferred_element_type=jnp.float32
            )
            + jnp.einsum("hts,shd->thd", grad_scores, keys_all, preferred_element_type=jnp.float32)
        )
        grad_key = att_scale * (
            jnp.einsum("she,hde->shd", values_all, later_bf, preferred_element_type=jnp.float32)
            + jnp.einsum("hts,thd->shd", grad_scores, queries, preferred_element_type=jnp.float32)
        )
        grad_value = att_scale * (
            jnp.einsum("shd,hde->she", keys_all, later_bf, preferred_element_type=jnp.float32)
            + jnp.einsum("hts,the->she", scores_bf, resid_bf, preferred_element_type=jnp.float32)
        )
        grad_blocks[block] = jnp.stack(
            [
                grad_query.reshape(BLK, head_width),
                grad_key.reshape(BLK, head_width),
                grad_value.reshape(BLK, head_width),
            ],
            0,
        ).astype(jnp.bfloat16)
    return grad_blocks[0]


def solution(mesh):
    in_specs = (
        P(None, ("grp", "ctx"), "role"),
        P("role", None),
        P(("role", "ctx"), None),
        P(("grp", "ctx")),
        P(),
        P(None, ("grp", "ctx"), "role"),
    )
    out_specs = P(None, ("grp", "ctx"), "role")
    return jax.shard_map(
        on_device, mesh=mesh, in_specs=in_specs, out_specs=out_specs, check_vma=False
    )
```

profile of v0, /device:TPU:0, one launch (start us, length us, event | category | flops | bytes accessed | tf_op | source)
XLA Modules:
  0.0 349.2 jit_solution(2665267496531229638)
XLA Ops:
  7.3 3.2 multiply_convert_fusion
  11.5 5.6 %collective-permute-start = (bf16[127,2048]{1,0:T(8,128)(2,1)}, bf16[127,2048]{1,0:T(8,128)(2,1)}, u32[]{:S(2)}, u32[]{:S(2)}) collective-permute-start(bf16[127,2048]{1,0:T(8,128)(2,1)} %slice_bitcast_fusion), channel_id=1, source_target_pairs={{0,1},{1,2},{2,3},{3,4},{4,5},{5,6},{6,7},{8,9},{9,10},{10,11},{11... | collective-permute-start | bytes 1560584 | tf_op jit(solution)/shard_map/ppermute | solution.py:14
  17.1 1.3 fusion.17
  21.0 1.5 rev.7
  23.4 3.0 fusion.42
  26.5 8.9 %collective-permute-done = bf16[127,2048]{1,0:T(8,128)(2,1)} collective-permute-done((bf16[127,2048]{1,0:T(8,128)(2,1)}, bf16[127,2048]{1,0:T(8,128)(2,1)}, u32[]{:S(2)}, u32[]{:S(2)}) %collective-permute-start) | collective-permute-done | bytes 520224 | tf_op jit(solution)/shard_map/ppermute | solution.py:14
  35.4 1.7 maximum_bitcast_fusion
  37.1 65.3 %fusion = bf16[1,512,2048]{2,0,1:T(2,128)(2,1)} fusion(bf16[128,1,2048]{2,1,0:T(2,128)(2,1)S(1)} %copy.85, bf16[1,639,2048]{2,1,0:T(8,128)(2,1)S(1)} %maximum_bitcast_fusion, bf16[1,512,2048]{2,1,0:T(8,128)(2,1)S(1)} %slice-done), kind=kOutput, calls=%fused_computation.5 | convolution fusion | flops 271581184 | bytes 7335936 | tf_op jit(solution)/shard_map/conv_general_dilated | solution.py:34
  102.4 40.9 %all-gather.6.cloned.1.call-done = bf16[2048,2048]{1,0:T(8,128)(2,1)} async-done(((bf16[256,2048]{1,0:T(8,128)(2,1)}), bf16[2048,2048]{1,0:T(8,128)(2,1)}) %all-gather.6.cloned.1.call-update) | async-done | bytes 8388624 | tf_op jit(solution)/shard_map/all_gather | solution.py:61
  143.2 11.5 %fusion.2 = f32[512,2048]{1,0:T(8,128)} fusion(bf16[2048,2048]{1,0:T(8,128)(2,1)} %all-gather.6.cloned.1.call-done, bf16[1,512,2048]{2,0,1:T(2,128)(2,1)} %fusion), kind=kOutput, calls=%fused_computation.11 | convolution fusion | flops 4294967296 | bytes 14680064 | tf_op jit(solution)/shard_map/dot_general | solution.py:63
  155.0 1.6 copy.113
  156.8 3.3 select_convert_fusion.1
  160.1 56.9 %all-gather.8.cloned.1.call-done = f32[64,128,128]{2,1,0:T(8,128)} async-done(((f32[8,128,128]{2,1,0:T(8,128)}), f32[64,128,128]{2,1,0:T(8,128)}) %all-gather.8.cloned.1.call-update) | async-done | bytes 4194320 | tf_op jit(solution)/shard_map/all_gather | solution.py:19
  217.0 8.8 %while.28 = (s32[]{:T(128)}, f32[8,128,128]{2,1,0:T(8,128)S(1)}, s32[]{:T(128)}, f32[8,8,128,128]{3,2,1,0:T(8,128)}, s32[]{:T(128)}, /*index=5*/s32[]{:T(128)}) while((s32[]{:T(128)}, f32[8,128,128]{2,1,0:T(8,128)S(1)}, s32[]{:T(128)}, f32[8,8,128,128]{3,2,1,0:T(8,128)}, s32[]{:T(128)}, /*index=5*/s32[]{:T(128)}) %tuple.75), condition=%wide.region_1.2_spmd.clone, body=%wide.region_0.1_spmd.clone.sunk | while | flops 393220 | bytes 1572965 | solution.py:29
  227.3 5.2 %fusion.9 = f32[512,8,128]{0,2,1:T(8,128)} fusion(f32[8,128,512]{2,1,0:T(8,128)S(1)} %fusion.15, bf16[8,512,512]{2,1,0:T(8,128)(2,1)} %select_convert_fusion.1, bf16[512,8,128]{0,2,1:T(8,128)(2,1)S(1)} %bitcast.79), kind=kOutput, calls=%fused_computation.21 | convolution fusion | flops 537919488 | bytes 9437184 | tf_op jit(solution)/shard_map/hts,she->the/dot_general | solution.py:86
  232.5 3.0 copy.86
  235.5 3.5 multiply_convert_fusion.2
  239.0 1.5 copy.114
  240.5 1.6 convolution_bitcast_fusion
  243.6 1.4 select_convert_fusion
  245.0 2.5 fusion.8
  247.5 2.3 copy.97
  249.7 4.4 %fusion.19 = f32[8,128,512]{2,1,0:T(8,128)} fusion(bf16[512,8,128]{0,2,1:T(8,128)(2,1)S(1)} %bitcast.85, bf16[8,512,512]{2,1,0:T(8,128)(2,1)} %select_convert_fusion.1), kind=kOutput, calls=%fused_computation.38 | convolution fusion | flops 536870912 | bytes 7340032 | tf_op jit(solution)/shard_map/hts,the->she/dot_general | solution.py:124
  254.2 61.3 %all-gather.10.cloned.1.call-done = f32[64,128,128]{2,1,0:T(8,128)} async-done(((f32[8,128,128]{2,1,0:T(8,128)}), f32[64,128,128]{2,1,0:T(8,128)}) %all-gather.10.cloned.1.call-update) | async-done | bytes 4194320 | tf_op jit(solution)/shard_map/all_gather | solution.py:19
  315.5 4.6 %rev.8 = f32[8,8,128,128]{3,2,1,0:T(8,128)} reverse(f32[8,8,128,128]{3,2,1,0:T(8,128)} %bitcast.95), dimensions={0} | reverse | bytes 8388608 | tf_op jit(solution)/shard_map/rev | solution.py:21
  320.1 8.7 %while.29 = (s32[]{:T(128)}, f32[8,128,128]{2,1,0:T(8,128)S(1)}, s32[]{:T(128)}, f32[8,8,128,128]{3,2,1,0:T(8,128)}, s32[]{:T(128)}, /*index=5*/s32[]{:T(128)}) while((s32[]{:T(128)}, f32[8,128,128]{2,1,0:T(8,128)S(1)}, s32[]{:T(128)}, f32[8,8,128,128]{3,2,1,0:T(8,128)}, s32[]{:T(128)}, /*index=5*/s32[]{:T(128)}) %tuple.64), condition=%wide.region_5.6_spmd.clone, body=%wide.region_4.5_spmd.clone.sunk | while | flops 393220 | bytes 1572965 | solution.py:29
  328.9 1.8 fusion.11
  331.5 1.5 multiply_convert_fusion.1
  333.0 1.5 copy.99
  334.5 4.7 %fusion.6 = bf16[512,8,128]{0,2,1:T(8,128)(2,1)} fusion(f32[8,128,512]{2,1,0:T(8,128)} %fusion.11, bf16[512,8,128]{0,2,1:T(8,128)(2,1)S(1)} %bitcast.89, bf16[8,512,512]{2,1,0:T(8,128)(2,1)} %copy-done.2), kind=kOutput, calls=%fused_computation.16 | convolution fusion | flops 538443776 | bytes 8388608 | tf_op jit(solution)/shard_map/hts,thd->shd/dot_general | solution.py:120
  339.2 1.5 copy.98
  340.7 2.0 pad_maximum_fusion
  (67 shorter events, 26.7 us)
Async XLA Ops:
  6.5 136.7 %all-gather.6.cloned.1.call-start = ((), (), s32[]{:S(2)}) async-start(), calls=%async_computation.1 | async-start | bytes 9437184 | tf_op jit(solution)/shard_map/all_gather | solution.py:61
  7.3 209.7 %all-gather.8.cloned.1.call-start = ((), (), s32[]{:S(2)}) async-start(), calls=%async_computation.3 | async-start | bytes 4718592 | tf_op jit(solution)/shard_map/all_gather | solution.py:19
  7.3 9.8 %copy-start.11 = (bf16[3,512,1024]{2,1,0:T(8,128)(2,1)S(1)}, bf16[3,512,1024]{2,1,0:T(8,128)(2,1)}, u32[]{:S(2)}) copy-start(bf16[3,512,1024]{2,1,0:T(8,128)(2,1)} %param.15) | copy-start | bytes 9437188
  11.5 23.9 %collective-permute-start = (bf16[127,2048]{1,0:T(8,128)(2,1)}, bf16[127,2048]{1,0:T(8,128)(2,1)}, u32[]{:S(2)}, u32[]{:S(2)}) collective-permute-start(bf16[127,2048]{1,0:T(8,128)(2,1)} %slice_bitcast_fusion), channel_id=1, source_target_pairs={{0,1},{1,2},{2,3},{3,4},{4,5},{5,6},{6,7},{8,9},{9,10},{10,11},{11... | collective-permute-start | bytes 1560584 | tf_op jit(solution)/shard_map/ppermute | solution.py:14
  18.9 1.9 copy-start
  19.5 1.3 copy-start.5
  19.5 1.5 copy-start.12
  20.8 214.7 %reduce-scatter.2.cloned.1.call-start = ((), (), s32[]{:S(2)}) async-start(), calls=%async_computation.2 | async-start | bytes 6291456 | tf_op jit(solution)/shard_map/reduce_scatter | solution.py:64
  26.4 10.7 %slice-start = ((bf16[3,512,2048]{2,1,0:T(8,128)(2,1)}), bf16[1,512,2048]{2,1,0:T(8,128)(2,1)S(1)}, s32[]{:S(2)}) async-start(bf16[3,512,2048]{2,1,0:T(8,128)(2,1)} %param.10), calls=%async_computation.5 | async-start | bytes 4194304 | tf_op jit(solution)/shard_map/slice | solution.py:51
  154.7 1.8 copy-start.13
  154.7 1.9 copy-start.14
  154.7 2.0 copy-start.6
  154.8 160.7 %all-gather.10.cloned.1.call-start = ((), (), s32[]{:S(2)}) async-start(), calls=%async_computation.4 | async-start | bytes 4718592 | tf_op jit(solution)/shard_map/all_gather | solution.py:19
  156.6 69.2 %copy-start.3 = (bf16[1,512,1024]{1,2,0:T(8,128)(2,1)}, bf16[1,512,1024]{1,2,0:T(8,128)(2,1)S(1)}, u32[]{:S(2)}) copy-start(bf16[1,512,1024]{1,2,0:T(8,128)(2,1)S(1)} %copy.113) | copy-start | bytes 3145732
  225.7 1.5 copy-start.1
  243.6 1.4 copy-start.7
  245.0 2.5 copy-start.2
  328.9 1.8 copy-start.8
  328.9 2.7 copy-start.9
  331.5 3.0 copy-start.4
  334.5 6.2 %copy-start.10 = (bf16[1,512,1024]{2,1,0:T(8,128)(2,1)S(1)}, bf16[1,512,1024]{2,1,0:T(8,128)(2,1)}, u32[]{:S(2)}) copy-start(bf16[1,512,1024]{2,1,0:T(8,128)(2,1)} %copy.97) | copy-start | bytes 3145732
Sparse Core Ops, SparseCore 0:
  9.5 133.6 all-gather.5
  145.3 71.5 all-gather.7
  219.2 10.2 reduce-scatter.1
  243.3 72.1 all-gather.9
where the time goes:
time: 350 us; the launch traced here: 349 us
  waiting for transfers between devices  169 us (48%)
  matrix products  105 us (30%)
  other arithmetic  30.7 us (9%)
  local copies, waits for them, and re-layouts  24.8 us (7%)
  between operations  13.5 us (4%)
  starting transfers between devices  5.94 us (2%)
    all_gather x2, waiting for transfers between devices, prefix(): pieces = lax.all_gather(value, axis)  118 us
    conv_general_dilated x1, matrix products, depthwise(): lax.conv_general_dilated(extended[None], kernel, (1,), 'VALID', dimension...  65.3 us
    all_gather x1, waiting for transfers between devices, on_device(): shard_rows = lax.all_gather(map_weight, 'ctx', axis=0, tiled=True)  40.9 us
    select_n x14, other arithmetic, turn(): return jnp.where(position < mine, longer, so_far)  17.2 us
    dot_general x1, matrix products, on_device(): jnp.dot(columns, shard_rows, preferred_element_type=jnp.float32)  11.5 us
    ppermute x1, waiting for transfers between devices, from_behind(): lax.ppermute(value, axis, [(source, source + steps) for source in range(l...  8.95 us
  transfers between devices with their start and end apart: 5, of which 4 were waited for; matrix products, arithmetic and copies ran while one was open for 36% of the time, Pallas kernels for 0%

commit v1 on v0

--- a/solution.py
+++ b/solution.py
@@ -6,6 +6,12 @@
 
 DH = 128
 BLK = 512
+
+
+def _close_points(vector, on_dim):
+    vector = jnp.moveaxis(vector, 0, on_dim)
+    w1 = vector.shape
+    return vector.reshape(*w1[:on_dim], w1[on_dim] * w1[on_dim + 1], *w1[on_dim + 2 :])
 
 
 def from_behind(value, axis, steps):
@@ -58,7 +64,21 @@
     conv_out = depthwise(jnp.concatenate([left_rim, mixed_in], 0), conv_filter)
     teacher_out = (gate_in.astype(jnp.float32) * conv_out).astype(jnp.bfloat16)
     zero_map = jnp.zeros((tok_rows, map_weight.shape[1]), jnp.float32)
-    shard_rows = lax.all_gather(map_weight, "ctx", axis=0, tiled=True)
+    n_lanes = jax.lax.axis_size("ctx")
+    rack = [(u, (u + 1) % n_lanes) for u in range(n_lanes)]
+    before, p_next = ([], [])
+    p = 0
+    by_place = [(no, src_i) for src_i, no in rack]
+    while p < n_lanes - 1:
+        if p % 2 == 0:
+            before.append(jax.lax.ppermute(before[-1] if before else map_weight, "ctx", rack))
+        else:
+            p_next.append(jax.lax.ppermute(p_next[-1] if p_next else map_weight, "ctx", by_place))
+        p += 1
+    met_up = jnp.stack([*before[::-1], map_weight, *p_next], 0)
+    r2 = jax.lax.axis_index("ctx") - len(before)
+    met_up = met_up[(jnp.arange(n_lanes) - r2) % n_lanes]
+    shard_rows = _close_points(met_up, 0)
     columns = lax.slice_in_dim(teacher_out, 0, shard_rows.shape[0], axis=1)
     partial_map = zero_map + jnp.dot(columns, shard_rows, preferred_element_type=jnp.float32)
     target = lax.psum_scatter(partial_map, "role", scatter_dimension=1, tiled=True)

time: 350 us -> 414 us (1.18)
  starting transfers between devices: 5.94 us -> 33.1 us
  local copies, waits for them, and re-layouts: 24.8 us -> 48.7 us
  waiting for transfers between devices: 169 us -> 179 us
    ppermute x0 -> x7, waiting for transfers between devices: none -> 116 us  [the longest x4 116 us: on_device(): jax.lax.ppermute(before[-1] if before else map_weight, 'ctx', rack)]
    all_gather x2, waiting for transfers between devices: 118 us -> 63.3 us  [prefix(): pieces = lax.all_gather(value, axis)]
    all_gather x1 -> x0, waiting for transfers between devices: 40.9 us -> none  [on_device(): shard_rows = lax.all_gather(map_weight, 'ctx', axis=0, tiled=True)]
    ppermute x0 -> x7, starting transfers between devices: none -> 30.4 us  [the longest x3 22.4 us: on_device(): jax.lax.ppermute(p_next[-1] if p_next else map_weight, 'ctx', by_place)]
    unnamed x32 -> x41, local copies, waits for them, and re-layouts: 4.23 us -> 16 us
    ppermute x1, waiting for transfers between devices: 8.95 us -> 0.01 us  [from_behind(): lax.ppermute(value, axis, [(source, source + steps) for source in range(l...]
    gather x0 -> x1, local copies, waits for them, and re-layouts: none -> 8.22 us  [on_device(): met_up = met_up[(jnp.arange(n_lanes) - r2) % n_lanes]]
  transfers between devices with their start and end apart: 5 -> 11, of which waited for: 4 -> 4; matrix products, arithmetic and copies ran while one was open for 36% -> 36% of each run, Pallas kernels for 0% -> 0%
where the time goes in v1:
time: 414 us; the launch traced here: 413 us
  waiting for transfers between devices  179 us (43%)
  matrix products  105 us (25%)
  local copies, waits for them, and re-layouts  48.7 us (12%)
  starting transfers between devices  33.1 us (8%)
  other arithmetic  31.8 us (8%)
  between operations  15.2 us (4%)
    ppermute x4, waiting for transfers between devices, on_device(): jax.lax.ppermute(before[-1] if before else map_weight, 'ctx', rack)  116 us
    conv_general_dilated x1, matrix products, depthwise(): lax.conv_general_dilated(extended[None], kernel, (1,), 'VALID', dimension...  65.1 us
    all_gather x2, waiting for transfers between devices, prefix(): pieces = lax.all_gather(value, axis)  63.3 us
    ppermute x3, starting transfers between devices, on_device(): jax.lax.ppermute(p_next[-1] if p_next else map_weight, 'ctx', by_place)  22.4 us
    select_n x14, other arithmetic, turn(): return jnp.where(position < mine, longer, so_far)  17.6 us
    unnamed x41, local copies, waits for them, and re-layouts  16 us
    dot_general x1, matrix products, on_device(): jnp.dot(columns, shard_rows, preferred_element_type=jnp.float32)  11.5 us
  transfers between devices with their start and end apart: 11, of which 4 were waited for; matrix products, arithmetic and copies ran while one was open for 36% of the time, Pallas kernels for 0%

profile of v1, /device:TPU:0, one launch (start us, length us, event | category | flops | bytes accessed | tf_op | source)
XLA Modules:
  0.0 412.9 jit_solution(14903009886015296770)
XLA Ops:
  7.4 2.9 collective-permute-start.1
  10.3 3.0 collective-permute-start.5
  13.3 3.2 fusion.19
  17.7 37.8 %collective-permute-done.1 = bf16[256,2048]{1,0:T(8,128)(2,1)} collective-permute-done((bf16[256,2048]{1,0:T(8,128)(2,1)}, bf16[256,2048]{1,0:T(8,128)(2,1)}, u32[]{:S(2)}, u32[]{:S(2)}) %collective-permute-start.1) | collective-permute-done | bytes 1048608 | tf_op jit(solution)/shard_map/ppermute | solution.py:74
  55.5 2.5 collective-permute-start.2
  59.3 3.0 multiply_convert_fusion
  63.3 2.6 collective-permute-start
  68.4 26.9 %collective-permute-done.2 = bf16[256,2048]{1,0:T(8,128)(2,1)S(1)} collective-permute-done((bf16[256,2048]{1,0:T(8,128)(2,1)}, bf16[256,2048]{1,0:T(8,128)(2,1)S(1)}, u32[]{:S(2)}, u32[]{:S(2)}) %collective-permute-start.2) | collective-permute-done | bytes 1048608 | tf_op jit(solution)/shard_map/ppermute | solution.py:74
  95.9 3.0 fusion.44
  99.6 5.2 %collective-permute-start.6 = (bf16[256,2048]{1,0:T(8,128)(2,1)}, bf16[256,2048]{1,0:T(8,128)(2,1)}, u32[]{:S(2)}, u32[]{:S(2)}) collective-permute-start(bf16[256,2048]{1,0:T(8,128)(2,1)} %collective-permute-done.5), channel_id=1, source_target_pairs={{1,0},{2,1},{3,2},{4,3},{5,4},{6,5},{7,6},{0,7},{9,8},{10,9},{11,1... | collective-permute-start | bytes 3145736 | tf_op jit(solution)/shard_map/ppermute | solution.py:76
  104.8 51.2 %collective-permute-done.3 = bf16[256,2048]{1,0:T(8,128)(2,1)} collective-permute-done((bf16[256,2048]{1,0:T(8,128)(2,1)S(1)}, bf16[256,2048]{1,0:T(8,128)(2,1)}, u32[]{:S(2)}, u32[]{:S(2)}) %collective-permute-start.3) | collective-permute-done | bytes 1048608 | tf_op jit(solution)/shard_map/ppermute | solution.py:74
  156.0 2.6 collective-permute-start.4
  158.6 65.1 %fusion = bf16[1,512,2048]{2,0,1:T(2,128)(2,1)} fusion(bf16[128,1,2048]{2,1,0:T(2,128)(2,1)S(1)} %copy.85, bf16[1,639,2048]{2,1,0:T(8,128)(2,1)S(1)} %maximum_bitcast_fusion, bf16[1,512,2048]{2,1,0:T(8,128)(2,1)S(1)} %slice-done), kind=kOutput, calls=%fused_computation.6 | convolution fusion | flops 271581184 | bytes 7335936 | tf_op jit(solution)/shard_map/conv_general_dilated | solution.py:40
  223.7 14.2 %collective-permute-start.7 = (bf16[256,2048]{1,0:T(8,128)(2,1)}, bf16[256,2048]{1,0:T(8,128)(2,1)S(1)}, u32[]{:S(2)}, u32[]{:S(2)}) collective-permute-start(bf16[256,2048]{1,0:T(8,128)(2,1)} %collective-permute-done.6), channel_id=1, source_target_pairs={{1,0},{2,1},{3,2},{4,3},{5,4},{6,5},{7,6},{0,7},{9,8},{10,9},{11,1... | collective-permute-start | bytes 3145736 | tf_op jit(solution)/shard_map/ppermute | solution.py:76
  237.9 2.4 bitcast_dynamic-update-slice_fusion.7
  243.6 2.3 bitcast_dynamic-update-slice_fusion.4
  252.8 8.2 %gather_fusion = bf16[8,256,2048]{2,1,0:T(8,128)(2,1)} fusion(bf16[8,256,2048]{2,1,0:T(8,128)(2,1)} %bitcast_dynamic-update-slice_fusion, s32[1024]{0:T(1024)} %pad_clamp_fusion), kind=kCustom, calls=%fused_computation | custom fusion | bytes 16777248 | tf_op jit(solution)/shard_map/gather | solution.py:80
  261.0 11.5 %fusion.2 = f32[512,2048]{1,0:T(8,128)} fusion(bf16[2048,2048]{1,0:T(8,128)(2,1)} %bitcast.113, bf16[1,512,2048]{2,0,1:T(2,128)(2,1)} %fusion), kind=kOutput, calls=%fused_computation.12 | convolution fusion | flops 4294967296 | bytes 14680064 | tf_op jit(solution)/shard_map/dot_general | solution.py:83
  274.4 3.3 select_convert_fusion.1
  277.8 9.1 %while.28 = (s32[]{:T(128)}, f32[8,128,128]{2,1,0:T(8,128)S(1)}, s32[]{:T(128)}, f32[8,8,128,128]{3,2,1,0:T(8,128)}, s32[]{:T(128)}, /*index=5*/s32[]{:T(128)}) while((s32[]{:T(128)}, f32[8,128,128]{2,1,0:T(8,128)S(1)}, s32[]{:T(128)}, f32[8,8,128,128]{3,2,1,0:T(8,128)}, s32[]{:T(128)}, /*index=5*/s32[]{:T(128)}) %tuple.73), condition=%wide.region_1.2_spmd.clone, body=%wide.region_0.1_spmd.clone.sunk | while | flops 393220 | bytes 1572957 | solution.py:35
  287.3 5.0 %fusion.9 = f32[512,8,128]{0,2,1:T(8,128)} fusion(f32[8,128,512]{2,1,0:T(8,128)S(1)} %fusion.15, bf16[8,512,512]{2,1,0:T(8,128)(2,1)} %select_convert_fusion.1, bf16[512,8,128]{0,2,1:T(8,128)(2,1)S(1)} %bitcast.98), kind=kOutput, calls=%fused_computation.22 | convolution fusion | flops 537919488 | bytes 9437184 | tf_op jit(solution)/shard_map/hts,she->the/dot_general | solution.py:106
  292.3 3.0 copy.86
  295.3 3.5 multiply_convert_fusion.2
  304.8 2.5 fusion.8
  309.6 4.4 %fusion.21 = f32[8,128,512]{2,1,0:T(8,128)} fusion(bf16[512,8,128]{0,2,1:T(8,128)(2,1)S(1)} %bitcast.104, bf16[8,512,512]{2,1,0:T(8,128)(2,1)} %select_convert_fusion.1), kind=kOutput, calls=%fused_computation.54 | convolution fusion | flops 536870912 | bytes 7340032 | tf_op jit(solution)/shard_map/hts,the->she/dot_general | solution.py:144
  314.0 63.3 %all-gather.7.cloned.1.call-done = f32[64,128,128]{2,1,0:T(8,128)} async-done(((f32[8,128,128]{2,1,0:T(8,128)}), f32[64,128,128]{2,1,0:T(8,128)}) %all-gather.7.cloned.1.call-update) | async-done | bytes 4194320 | tf_op jit(solution)/shard_map/all_gather | solution.py:25
  377.3 4.6 %rev.8 = f32[8,8,128,128]{3,2,1,0:T(8,128)} reverse(f32[8,8,128,128]{3,2,1,0:T(8,128)} %bitcast.115), dimensions={0} | reverse | bytes 8388608 | tf_op jit(solution)/shard_map/rev | solution.py:27
  382.0 8.8 %while.29 = (s32[]{:T(128)}, f32[8,128,128]{2,1,0:T(8,128)S(1)}, s32[]{:T(128)}, f32[8,8,128,128]{3,2,1,0:T(8,128)}, s32[]{:T(128)}, /*index=5*/s32[]{:T(128)}) while((s32[]{:T(128)}, f32[8,128,128]{2,1,0:T(8,128)S(1)}, s32[]{:T(128)}, f32[8,8,128,128]{3,2,1,0:T(8,128)}, s32[]{:T(128)}, /*index=5*/s32[]{:T(128)}) %tuple.64), condition=%wide.region_5.6_spmd.clone, body=%wide.region_4.5_spmd.clone.sunk | while | flops 393220 | bytes 1572957 | solution.py:35
  391.2 4.1 fusion.6
  395.3 2.4 copy.98
  397.7 3.1 multiply_convert_fusion.1
  402.2 3.2 pad_maximum_fusion
  (91 shorter events, 47.4 us)
Async XLA Ops:
  7.4 270.4 %all-gather.5.cloned.1.call-start = ((), (), s32[]{:S(2)}) async-start(), calls=%async_computation.2 | async-start | bytes 4718592 | tf_op jit(solution)/shard_map/all_gather | solution.py:25
  7.4 48.1 %collective-permute-start.1 = (bf16[256,2048]{1,0:T(8,128)(2,1)}, bf16[256,2048]{1,0:T(8,128)(2,1)}, u32[]{:S(2)}, u32[]{:S(2)}) collective-permute-start(bf16[256,2048]{1,0:T(8,128)(2,1)} %param.12), channel_id=1, source_target_pairs={{0,1},{1,2},{2,3},{3,4},{4,5},{5,6},{6,7},{7,0},{8,9},{9,10},{10,1... | collective-permute-start | bytes 3145736 | tf_op jit(solution)/shard_map/ppermute | solution.py:74
  10.3 89.3 %collective-permute-start.5 = (bf16[256,2048]{1,0:T(8,128)(2,1)}, bf16[256,2048]{1,0:T(8,128)(2,1)}, u32[]{:S(2)}, u32[]{:S(2)}) collective-permute-start(bf16[256,2048]{1,0:T(8,128)(2,1)} %param.12), channel_id=1, source_target_pairs={{1,0},{2,1},{3,2},{4,3},{5,4},{6,5},{7,6},{0,7},{9,8},{10,9},{11,1... | collective-permute-start | bytes 3145736 | tf_op jit(solution)/shard_map/ppermute | solution.py:76
  17.1 45.2 %copy-start.5 = (bf16[1,512,1024]{1,2,0:T(8,128)(2,1)}, bf16[1,512,1024]{1,2,0:T(8,128)(2,1)S(1)}, u32[]{:S(2)}) copy-start(bf16[1,512,1024]{1,2,0:T(8,128)(2,1)S(1)} %copy.75) | copy-start | bytes 3145732
  17.7 44.7 %copy-start = (bf16[1,512,1024]{1,2,0:T(8,128)(2,1)}, bf16[1,512,1024]{1,2,0:T(8,128)(2,1)S(1)}, u32[]{:S(2)}) copy-start(bf16[1,512,1024]{1,2,0:T(8,128)(2,1)S(1)} %copy.112) | copy-start | bytes 3145732
  55.5 39.7 %collective-permute-start.2 = (bf16[256,2048]{1,0:T(8,128)(2,1)}, bf16[256,2048]{1,0:T(8,128)(2,1)S(1)}, u32[]{:S(2)}, u32[]{:S(2)}) collective-permute-start(bf16[256,2048]{1,0:T(8,128)(2,1)} %collective-permute-done.1), channel_id=1, source_target_pairs={{0,1},{1,2},{2,3},{3,4},{4,5},{5,6},{6,7},{7,0},{8,9},{9,10},{10,1... | collective-permute-start | bytes 3145736 | tf_op jit(solution)/shard_map/ppermute | solution.py:74
  59.3 236.1 %reduce-scatter.2.cloned.1.call-start = ((), (), s32[]{:S(2)}) async-start(), calls=%async_computation.1 | async-start | bytes 6291456 | tf_op jit(solution)/shard_map/reduce_scatter | solution.py:84
  63.3 2.6 copy-start.13
  63.3 35.6 %collective-permute-start = (bf16[127,2048]{1,0:T(8,128)(2,1)}, bf16[127,2048]{1,0:T(8,128)(2,1)S(1)}, u32[]{:S(2)}, u32[]{:S(2)}) collective-permute-start(bf16[127,2048]{1,0:T(8,128)(2,1)} %slice_bitcast_fusion), channel_id=1, source_target_pairs={{0,1},{1,2},{2,3},{3,4},{4,5},{5,6},{6,7},{8,9},{9,10},{10,11},{11... | collective-permute-start | bytes 1560584 | tf_op jit(solution)/shard_map/ppermute | solution.py:20
  95.2 4.3 %copy-start.11 = (bf16[256,2048]{1,0:T(8,128)(2,1)}, bf16[256,2048]{1,0:T(8,128)(2,1)S(1)}, u32[]{:S(2)}) copy-start(bf16[256,2048]{1,0:T(8,128)(2,1)S(1)} %collective-permute-done.2) | copy-start | bytes 3145732
  95.2 60.7 %collective-permute-start.3 = (bf16[256,2048]{1,0:T(8,128)(2,1)S(1)}, bf16[256,2048]{1,0:T(8,128)(2,1)}, u32[]{:S(2)}, u32[]{:S(2)}) collective-permute-start(bf16[256,2048]{1,0:T(8,128)(2,1)S(1)} %collective-permute-done.2), channel_id=1, source_target_pairs={{0,1},{1,2},{2,3},{3,4},{4,5},{5,6},{6,7},{7,0},{8,9},{9,10},{10,1... | collective-permute-start | bytes 3145736 | tf_op jit(solution)/shard_map/ppermute | solution.py:74
  98.9 59.7 %slice-start = ((bf16[3,512,2048]{2,1,0:T(8,128)(2,1)}), bf16[1,512,2048]{2,1,0:T(8,128)(2,1)S(1)}, s32[]{:S(2)}) async-start(bf16[3,512,2048]{2,1,0:T(8,128)(2,1)} %param.10), calls=%async_computation.4 | async-start | bytes 4194304 | tf_op jit(solution)/shard_map/slice | solution.py:57
  99.6 124.1 %collective-permute-start.6 = (bf16[256,2048]{1,0:T(8,128)(2,1)}, bf16[256,2048]{1,0:T(8,128)(2,1)}, u32[]{:S(2)}, u32[]{:S(2)}) collective-permute-start(bf16[256,2048]{1,0:T(8,128)(2,1)} %collective-permute-done.5), channel_id=1, source_target_pairs={{1,0},{2,1},{3,2},{4,3},{5,4},{6,5},{7,6},{0,7},{9,8},{10,9},{11,1... | collective-permute-start | bytes 3145736 | tf_op jit(solution)/shard_map/ppermute | solution.py:76
  156.0 81.9 %collective-permute-start.4 = (bf16[256,2048]{1,0:T(8,128)(2,1)}, bf16[256,2048]{1,0:T(8,128)(2,1)}, u32[]{:S(2)}, u32[]{:S(2)}) collective-permute-start(bf16[256,2048]{1,0:T(8,128)(2,1)} %collective-permute-done.3), channel_id=1, source_target_pairs={{0,1},{1,2},{2,3},{3,4},{4,5},{5,6},{6,7},{7,0},{8,9},{9,10},{10,1... | collective-permute-start | bytes 3145736 | tf_op jit(solution)/shard_map/ppermute | solution.py:74
  223.7 18.9 %copy-start.12 = (bf16[256,2048]{1,0:T(8,128)(2,1)S(1)}, bf16[256,2048]{1,0:T(8,128)(2,1)}, u32[]{:S(2)}) copy-start(bf16[256,2048]{1,0:T(8,128)(2,1)} %copy-done.11) | copy-start | bytes 3145732
  223.7 22.3 %copy-start.10 = (bf16[256,2048]{1,0:T(8,128)(2,1)S(1)}, bf16[256,2048]{1,0:T(8,128)(2,1)}, u32[]{:S(2)}) copy-start(bf16[256,2048]{1,0:T(8,128)(2,1)} %param.12) | copy-start | bytes 3145732
  223.7 28.0 %collective-permute-start.7 = (bf16[256,2048]{1,0:T(8,128)(2,1)}, bf16[256,2048]{1,0:T(8,128)(2,1)S(1)}, u32[]{:S(2)}, u32[]{:S(2)}) collective-permute-start(bf16[256,2048]{1,0:T(8,128)(2,1)} %collective-permute-done.6), channel_id=1, source_target_pairs={{1,0},{2,1},{3,2},{4,3},{5,4},{6,5},{7,6},{0,7},{9,8},{10,9},{11,1... | collective-permute-start | bytes 3145736 | tf_op jit(solution)/shard_map/ppermute | solution.py:76
  272.5 1.7 copy-start.14
  272.5 1.7 copy-start.15
  272.5 1.9 copy-start.6
  272.6 104.8 %all-gather.7.cloned.1.call-start = ((), (), s32[]{:S(2)}) async-start(), calls=%async_computation.3 | async-start | bytes 4718592 | tf_op jit(solution)/shard_map/all_gather | solution.py:25
  274.2 12.6 %copy-start.3 = (bf16[1,512,1024]{1,2,0:T(8,128)(2,1)}, bf16[1,512,1024]{1,2,0:T(8,128)(2,1)S(1)}, u32[]{:S(2)}) copy-start(bf16[1,512,1024]{1,2,0:T(8,128)(2,1)S(1)} %copy.113) | copy-start | bytes 3145732
  277.7 9.6 %copy-start.1 = (bf16[1,512,1024]{1,2,0:T(8,128)(2,1)S(1)}, bf16[1,512,1024]{1,2,0:T(8,128)(2,1)}, u32[]{:S(2)}) copy-start(bf16[1,512,1024]{1,2,0:T(8,128)(2,1)} %copy-done) | copy-start | bytes 3145732
  303.4 1.4 copy-start.7
  304.8 2.5 copy-start.2
  382.0 9.3 %copy-start.4 = (bf16[1,512,1024]{1,2,0:T(8,128)(2,1)S(1)}, bf16[1,512,1024]{1,2,0:T(8,128)(2,1)}, u32[]{:S(2)}) copy-start(bf16[1,512,1024]{1,2,0:T(8,128)(2,1)} %copy-done.3) | copy-start | bytes 3145732
  391.2 6.4 %copy-start.8 = (bf16[1,512,1024]{1,2,0:T(8,128)(2,1)S(1)}, bf16[1,512,1024]{1,2,0:T(8,128)(2,1)}, u32[]{:S(2)}) copy-start(bf16[1,512,1024]{1,2,0:T(8,128)(2,1)} %copy-done.5) | copy-start | bytes 3145732
  395.3 6.9 %copy-start.9 = (bf16[1,512,1024]{2,1,0:T(8,128)(2,1)S(1)}, bf16[1,512,1024]{2,1,0:T(8,128)(2,1)}, u32[]{:S(2)}) copy-start(bf16[1,512,1024]{2,1,0:T(8,128)(2,1)} %copy.97) | copy-start | bytes 3145732
Sparse Core Ops, SparseCore 0:
  59.4 153.7 all-gather.4
  303.1 74.1 all-gather.6
Sparse Core Ops, SparseCore 1:
  272.6 12.6 reduce-scatter.1
